TPU v7x, 32 devices: a whole 2x2x4 slice. The times are simulated.
32 devices in a mesh: dp: 8 (over z, y), ctx: 4 (over x, core).
Axes of the slice: x: 2, y: 2, z: 4, core: 2. Of those that a mesh axis runs over, the one named last changes fastest.
Arguments:
- tokens: bfloat16 [4096, 1024], P(('dp', 'ctx')), parts along dimension 0, may hold values from -6 to 6
- queries: bfloat16 [4096, 1024], P(('dp', 'ctx')), parts along dimension 0, may hold values from -128 to 128
- key_weight: bfloat16 [1024, 1024], replicated, may hold values from -0.1875 to 0.1875
- value_weight: bfloat16 [1024, 1024], replicated, may hold values from -0.1875 to 0.1875
- lengths: int32 [48], P('dp'), parts along dimension 0, may hold values from 1 to 256, 512 in all
- dest_slot: int32 [128], P('dp'), parts along dimension 0, may hold values from 0 to 15, as said below
- block_mask: int32 [128, 16], P('dp'), parts along dimension 0, may hold values 0 or 1
Outputs:
- attended: bfloat16 [4096, 1024], P(('dp', 'ctx')), parts along dimension 0
There are 8 independent parts, one for each index of `dp`. A program takes and returns all parts, laid end to end along the dimension named above; an argument that names none is the same for every part. Nothing has to cross between parts.
Inputs may be any that keep to these rules, and one draw needn't show every extreme that they name: dest_slot is a permutation of the 16 slots; slot r lies on device r // 4. The 4 blocks that start on one device go in two pairs to two different devices, so every device receives exactly 2 blocks from each of two devices.
All inputs are finite; a program needn't handle non-finite values.
Results may differ from a plain program's by a relative error of at most 0.012.
The roundings to bfloat16 on the way count: a program that leaves them out, or rounds other values in their place, can miss the bound.
Values may be sent and summed in bfloat16 or wider, within the bound.
A program may use at most 64 MiB of HBM per device.

v0:
```python
import jax
import jax.numpy as jnp
from jax import lax
from jax.sharding import PartitionSpec as P

HEADS = 8
HD = 128
BLOCKS_DEV = 4


def clip_index(position, lengths):
    bounds = jnp.cumsum(lengths)
    return jnp.sum((position[:, None] >= bounds[None, :]).astype(jnp.int32), axis=1)


def collect_rows(wanted, carry, pieces):
    count = pieces[0].shape[0]
    inside = (wanted >= 0) & (wanted < count)
    position = jnp.clip(wanted, 0, count - 1)
    return tuple(
        (
            jnp.where(inside[:, None], jnp.take(piece, position, axis=0), kept)
            for piece, kept in zip(pieces, carry)
        )
    )


def on_device(tokens, queries, key_weight, value_weight, lengths, dest_slot, block_mask):
    device_id = lax.axis_index("ctx")
    row_count = tokens.shape[0]
    inner_width = queries.shape[1]
    block_rows = row_count // BLOCKS_DEV
    block_count = dest_slot.shape[0]
    block_ids = jnp.arange(block_count, dtype=jnp.int32)
    source_block = jnp.zeros((block_count,), jnp.int32).at[dest_slot].set(block_ids)
    my_slots = device_id * BLOCKS_DEV + jnp.arange(BLOCKS_DEV, dtype=jnp.int32)
    mine = source_block[my_slots]
    offsets = jnp.arange(block_rows, dtype=jnp.int32)
    wanted = (mine[:, None] * block_rows + offsets[None, :]).reshape(row_count)
    start_rows = (jnp.zeros_like(tokens), jnp.zeros_like(queries))
    moved_tokens, moved_queries = collect_rows(
        wanted,
        start_rows,
        (
            lax.all_gather(tokens, "ctx", axis=0, tiled=True),
            lax.all_gather(queries, "ctx", axis=0, tiled=True),
        ),
    )
    key_rows = jnp.dot(moved_tokens, key_weight, preferred_element_type=jnp.float32).astype(
        jnp.bfloat16
    )
    value_rows = jnp.dot(moved_tokens, value_weight, preferred_element_type=jnp.float32).astype(
        jnp.bfloat16
    )
    query_clip = clip_index(wanted, lengths)
    query_block_id = wanted // block_rows
    onehot_query = (query_block_id[:, None] == block_ids[None, :]).astype(jnp.float32)
    mask_rows = jnp.dot(onehot_query, block_mask.astype(jnp.float32))
    query_three = moved_queries.reshape(row_count, HEADS, HD)
    score_scale = 1.0 / HD**0.5
    key_piece = lax.all_gather(key_rows, "ctx", axis=0, tiled=True)
    value_piece = lax.all_gather(value_rows, "ctx", axis=0, tiled=True)
    count = key_piece.shape[0]
    key_slot = jnp.arange(count, dtype=jnp.int32)
    key_block = source_block[key_slot // block_rows]
    key_pos = key_block * block_rows + key_slot % block_rows
    key_clip = clip_index(key_pos, lengths)
    onehot_key = (block_ids[:, None] == key_block[None, :]).astype(jnp.float32)
    linked = jnp.dot(mask_rows, onehot_key) > 0.5
    allowed = (query_clip[:, None] == key_clip[None, :]) & (
        (query_block_id[:, None] == key_block[None, :]) | linked
    )
    scores = (
        jnp.einsum(
            "qhd,khd->hqk",
            query_three,
            key_piece.reshape(count, HEADS, HD),
            preferred_element_type=jnp.float32,
        )
        * score_scale
    )
    run_max = jnp.full((HEADS, row_count), -1e30, jnp.float32)
    run_acc = jnp.zeros((row_count, HEADS, HD), jnp.float32)
    masked = jnp.where(allowed[None], scores, jnp.float32(-1e30))
    new_max = jnp.maximum(run_max, jnp.max(masked, axis=-1))
    rescale = jnp.exp(run_max - new_max)
    weights_exp = jnp.where(allowed[None], jnp.exp(masked - new_max[..., None]), jnp.float32(0.0))
    new_total = jnp.sum(weights_exp, axis=-1)
    partial_value = jnp.einsum(
        "hqk,khd->qhd",
        weights_exp.astype(jnp.bfloat16),
        value_piece.reshape(count, HEADS, HD),
        preferred_element_type=jnp.float32,
    )
    new_acc = run_acc * rescale.T[:, :, None] + partial_value
    finished = (
        (new_acc / new_total.T[:, :, None]).reshape(row_count, inner_width).astype(jnp.bfloat16)
    )
    return finished


def solution(mesh):
    placed = (
        P(("dp", "ctx"), None),
        P(("dp", "ctx"), None),
        P(),
        P(),
        P("dp"),
        P("dp"),
        P("dp", None),
    )
    return jax.shard_map(
        on_device, mesh=mesh, in_specs=placed, out_specs=P(("dp", "ctx"), None), check_vma=False
    )
```

profile of v0, /device:TPU:1, one launch (start us, length us, event | category | flops | bytes accessed | tf_op | source)
XLA Modules:
  0.0 94.3 jit_solution(11212284214255987302)
XLA Ops:
  6.5 0.0 copy-start
  6.5 0.0 all-gather.7.cloned.1.call-start
  6.5 0.7 all-gather.7.cloned.1.call-update
  7.3 0.0 all-gather.5.cloned.1.call-start
  7.3 0.7 all-gather.5.cloned.1.call-update
  8.0 0.0 all-gather.9.cloned.1.call-start
  8.1 0.7 compare_select_fusion.9
  8.7 0.6 scatter_custom_fusion
  9.4 0.6 gather_fusion
  10.0 0.1 iota_add_fusion
  10.1 0.1 add.112
  10.2 0.0 copy-start.3
  10.2 17.9 %all-gather.7.cloned.1.call-done = bf16[512,1024]{1,0:T(8,128)(2,1)} async-done(((bf16[128,1024]{1,0:T(8,128)(2,1)}), bf16[512,1024]{1,0:T(8,128)(2,1)}) %all-gather.7.cloned.1.call-update) | async-done | bytes 1048592 | tf_op jit(solution)/shard_map/all_gather | solution.py:45
  28.2 2.4 %gather_fusion.2 = bf16[128,1024]{1,0:T(8,128)(2,1)S(1)} fusion(bf16[512,1024]{1,0:T(8,128)(2,1)} %all-gather.7.cloned.1.call-done, s32[1024]{0:T(1024)S(1)} %pad_clamp_fusion), kind=kCustom, calls=%fused_computation.1.clone | custom fusion | bytes 524800 | tf_op jit(solution)/shard_map/jit(_take)/gather | solution.py:22
  30.6 0.0 copy-done
  30.6 1.3 %convolution_convert_fusion.1 = bf16[128,1024]{1,0:T(8,128)(2,1)} fusion(bf16[1024,1024]{1,0:T(8,128)(2,1)S(1)} %copy-done, bf16[128,1024]{1,0:T(8,128)(2,1)S(1)} %gather_fusion.2, pred[128]{0:T(512)(128)(4,1)S(1)} %get-tuple-element.8, pred[128]{0:T(512)(128)(4,1)S(1)} %get-tuple-element.28), kind=kOutput, calls=%fused_computation.14 | convolution fusion | flops 268828672 | bytes 2621696 | tf_op jit(solution)/shard_map/dot_general | solution.py:49
  31.8 0.0 copy-start.2
  31.8 0.0 all-gather.9.cloned.1.call-update
  31.9 0.0 all-gather.11.cloned.1.call-start
  31.9 0.0 copy-done.3
  31.9 0.2 reduce-window.8
  32.4 0.7 fusion.37
  33.1 4.3 %compare_select_fusion.1 = s32[512,1]{0,1:T(1,128)S(1)} fusion(s32[]{:T(128)} %bitcast.12, s32[]{:T(128)} %bitcast.13, s32[]{:T(128)} %bitcast.14, s32[]{:T(128)} %bitcast.15, s32[]{:T(128)} %bitcast.16, s32[]{:T(128)} %bitcast.18, s32[]{:T(128)} %bitcast.17), kind=kLoop, calls=%fused_computation.48 | loop fusion | flops 11776 | bytes 2076 | tf_op jit(solution)/shard_map/gather | solution.py:65
  37.4 0.1 convert_reduce_fusion.1
  37.5 2.8 %convolution_convert_fusion = bf16[128,1024]{1,0:T(8,128)(2,1)} fusion(bf16[1024,1024]{1,0:T(8,128)(2,1)} %param.12, bf16[128,1024]{1,0:T(8,128)(2,1)S(1)} %gather_fusion.2, pred[128]{0:T(512)(128)(4,1)S(1)} %get-tuple-element.8, pred[128]{0:T(512)(128)(4,1)S(1)} %get-tuple-element.28), kind=kOutput, calls=%fused_computation.13 | convolution fusion | flops 268828672 | bytes 2621696 | tf_op jit(solution)/shard_map/dot_general | solution.py:52
  40.3 0.0 all-gather.11.cloned.1.call-update
  40.3 5.6 %fusion.27 = (s32[512]{0:T(512)S(1)}, s32[512]{0:T(512)S(1)}) fusion(pred[512]{0:T(512)(128)(4,1)S(1)} %compare_reduce_fusion, pred[512]{0:T(512)(128)(4,1)S(1)} %compare_reduce_fusion.1, pred[512]{0:T(512)(128)(4,1)S(1)} %compare_reduce_fusion.2, pred[512]{0:T(512)(128)(4,1)S(1)} %compare_reduce_fusion.3, pred[512]{0:T(512)(128)(4,1)S(1)} %compare_reduce_fusion.4, ...), kind=kLoop, calls=%fused_computation.66 | loop fusion | flops 8704 | bytes 10788 | tf_op jit(solution)/shard_map/add | solution.py:66
  46.0 0.1 convert_reduce_fusion
  46.1 0.0 copy-done.2
  46.1 0.5 fusion.7
  46.6 0.0 all-gather.5.cloned.1.call-done
  46.6 2.4 %gather_fusion.1 = bf16[128,1024]{1,0:T(8,128)(2,1)S(1)} fusion(bf16[512,1024]{1,0:T(8,128)(2,1)} %all-gather.5.cloned.1.call-done, s32[1024]{0:T(1024)S(1)} %pad_clamp_fusion), kind=kCustom, calls=%fused_computation.clone | custom fusion | bytes 524800 | tf_op jit(solution)/shard_map/jit(_take)/gather | solution.py:22
  49.0 15.9 %all-gather.9.cloned.1.call-done = bf16[512,1024]{1,0:T(8,128)(2,1)} async-done(((bf16[128,1024]{1,0:T(8,128)(2,1)}), bf16[512,1024]{1,0:T(8,128)(2,1)}) %all-gather.9.cloned.1.call-update) | async-done | bytes 1048592 | tf_op jit(solution)/shard_map/all_gather | solution.py:61
  64.9 1.9 %fusion = (f32[8,128]{1,0:T(8,128)S(1)}, f32[8,128,512]{2,1,0:T(8,128)S(1)}) fusion(pred[128,512]{1,0:T(8,128)(4,1)S(1)} %fusion.7, bf16[512,1024]{1,0:T(8,128)(2,1)} %all-gather.9.cloned.1.call-done, bf16[128,1024]{1,0:T(8,128)(2,1)S(1)} %gather_fusion.1, pred[128]{0:T(512)(128)(4,1)S(1)} %get-tuple-element.8, pred[128]{0:T(512)(128)(4,1)S(1)} %get-tuple-element.28), kind=kOutput, calls=%fused_computation.6 | convolution fusion | flops 136051712 | bytes 3477760 | tf_op jit(solution)/shard_map/qhd,khd->hqk/dot_general | solution.py:74
  66.8 0.0 copy-start.1
  66.8 1.3 %copy-done.1 = f32[8,128,512]{2,1,0:T(8,128)} copy-done((f32[8,128,512]{2,1,0:T(8,128)}, f32[8,128,512]{2,1,0:T(8,128)S(1)}, u32[]{:S(2)}) %copy-start.1) | copy-done | bytes 2097176
  68.1 0.7 fusion.1
  68.8 14.2 %all-gather.11.cloned.1.call-done = bf16[512,1024]{1,0:T(8,128)(2,1)} async-done(((bf16[128,1024]{1,0:T(8,128)(2,1)}), bf16[512,1024]{1,0:T(8,128)(2,1)}) %all-gather.11.cloned.1.call-update) | async-done | bytes 1048592 | tf_op jit(solution)/shard_map/all_gather | solution.py:62
  83.1 1.5 %copy.20 = bf16[512,1024]{0,1:T(8,128)(2,1)S(1)} copy(bf16[512,1024]{1,0:T(8,128)(2,1)} %all-gather.11.cloned.1.call-done) | data formatting | bytes 2097152 | tf_op jit(solution)/shard_map/reshape | solution.py:92
  84.6 2.3 %fusion.5 = bf16[128,8,128]{0,2,1:T(8,128)(2,1)S(1)} fusion(bf16[512,8,128]{0,2,1:T(8,128)(2,1)S(1)} %bitcast.55, f32[8,128,512]{2,1,0:T(8,128)} %copy-done.1, f32[8,128]{1,0:T(8,128)S(1)} %get-tuple-element.11, pred[128,512]{1,0:T(8,128)(4,1)S(1)} %fusion.7, f32[128,8]{0,1:T(8,128)S(1)} %bitcast.58, f32[128,8]{0,1:T(8,128)S(1)} %get-tuple-element.10), kind=kOutput, calls=%fused_computation.12 | convolution fusion | flops 137232384 | bytes 3485696 | tf_op jit(solution)/shard_map/hqk,khd->qhd/dot_general | solution.py:89
  86.9 0.9 copy.19
  (17 shorter events, 0.4 us)
Async XLA Ops:
  6.5 24.0 %copy-start = (bf16[1024,1024]{1,0:T(8,128)(2,1)S(1)}, bf16[1024,1024]{1,0:T(8,128)(2,1)}, u32[]{:S(2)}) copy-start(bf16[1024,1024]{1,0:T(8,128)(2,1)} %param.11) | copy-start | bytes 6291460
  6.5 21.6 %all-gather.7.cloned.1.call-start = ((), (), s32[]{:S(2)}) async-start(), calls=%async_computation.1 | async-start | bytes 1310720 | tf_op jit(solution)/shard_map/all_gather | solution.py:45
  7.3 39.3 %all-gather.5.cloned.1.call-start = ((), (), s32[]{:S(2)}) async-start(), calls=%async_computation | async-start | bytes 1310720 | tf_op jit(solution)/shard_map/all_gather | solution.py:46
  8.0 56.9 %all-gather.9.cloned.1.call-start = ((), (), s32[]{:S(2)}) async-start(), calls=%async_computation.2 | async-start | bytes 1310720 | tf_op jit(solution)/shard_map/all_gather | solution.py:61
  10.2 21.7 %copy-start.3 = (s32[6]{0:T(128)S(1)}, s32[6]{0:T(128)}, u32[]{:S(2)}) copy-start(s32[6]{0:T(128)} %param.13) | copy-start | bytes 76
  31.8 14.3 %copy-start.2 = (s32[16,16]{1,0:T(8,128)S(1)}, s32[16,16]{1,0:T(8,128)}, u32[]{:S(2)}) copy-start(s32[16,16]{1,0:T(8,128)} %param.15) | copy-start | bytes 3076
  31.9 51.2 %all-gather.11.cloned.1.call-start = ((), (), s32[]{:S(2)}) async-start(), calls=%async_computation.3 | async-start | bytes 1310720 | tf_op jit(solution)/shard_map/all_gather | solution.py:62
  66.8 1.4 %copy-start.1 = (f32[8,128,512]{2,1,0:T(8,128)}, f32[8,128,512]{2,1,0:T(8,128)S(1)}, u32[]{:S(2)}) copy-start(f32[8,128,512]{2,1,0:T(8,128)S(1)} %get-tuple-element.30) | copy-start | bytes 6291460
Sparse Core Ops, SparseCore 0:
  8.9 19.1 all-gather.6
  29.7 16.7 all-gather.4
  48.1 16.7 all-gather.8
  66.3 16.7 all-gather.10
where the time goes:
time: 95 us; the launch traced here: 94.3 us
  waiting for transfers between devices  49.5 us (52%)
  between operations  13.3 us (14%)
  other arithmetic  12.1 us (13%)
  local copies, waits for them, and re-layouts  10.6 us (11%)
  matrix products  8.77 us (9%)
    all_gather x1, waiting for transfers between devices, on_device(): lax.all_gather(tokens, 'ctx', axis=0, tiled=True)  17.9 us
    all_gather x1, waiting for transfers between devices, on_device(): key_piece = lax.all_gather(key_rows, 'ctx', axis=0, tiled=True)  15.9 us
    all_gather x1, waiting for transfers between devices, on_device(): value_piece = lax.all_gather(value_rows, 'ctx', axis=0, tiled=True)  14.2 us
    add x1, other arithmetic, on_device(): key_pos = key_block * block_rows + key_slot % block_rows  5.64 us
    gather x2, local copies, waits for them, and re-layouts, collect_rows(): jnp.take(piece, position, axis=0)  4.8 us
    gather x10, other arithmetic, on_device(): key_block = source_block[key_slot // block_rows]  4.6 us
    dot_general x1, matrix products, on_device(): jnp.dot(moved_tokens, value_weight, preferred_element_type=jnp.float32)  2.82 us
    dot_general x1, matrix products, on_device(): jnp.einsum('hqk,khd->qhd', weights_exp.astype(jnp.bfloat16), value_piece....  2.33 us
  transfers between devices with their start and end apart: 4, of which 3 were waited for; matrix products, arithmetic and copies ran while one was open for 27% of the time, Pallas kernels for 0%

commit v1 on v0

--- a/solution.py
+++ b/solution.py
@@ -1,6 +1,8 @@
 import jax
 import jax.numpy as jnp
 from jax import lax
+from jax.experimental import pallas as pl
+from jax.experimental.pallas import tpu as pltpu
 from jax.sharding import PartitionSpec as P
 
 HEADS = 8
@@ -9,7 +11,8 @@
 
 
 def clip_index(position, lengths):
-    bounds = jnp.cumsum(lengths)
+    order = jnp.arange(lengths.shape[0], dtype=jnp.int32)
+    bounds = jnp.sum(jnp.where(order[None, :] <= order[:, None], lengths[None, :], 0), axis=1)
     return jnp.sum((position[:, None] >= bounds[None, :]).astype(jnp.int32), axis=1)
 
 
@@ -99,6 +102,309 @@
     return finished
 
 
+TOK_CHUNKS = 4
+Q_CHUNKS = 2
+LOG2E = 1.4426950408889634
+
+
+def fused_kernel(
+    dest,
+    lengths,
+    mask_ref,
+    tok_hbm,
+    q_hbm,
+    kw_hbm,
+    vw_hbm,
+    out_ref,
+    tok,
+    q_own,
+    q_send,
+    q_all,
+    kw,
+    vw,
+    keys,
+    values,
+    linked,
+    result,
+    load_sem,
+    tok_send,
+    tok_recv,
+    relay_send,
+    relay_recv,
+    near_send,
+    near_recv,
+    q_ssem,
+    q_rsem,
+):
+    rows, width = tok_hbm.shape
+    block_rows = rows // BLOCKS_DEV
+    seq = 4 * rows
+    blocks = 4 * BLOCKS_DEV
+    heads = width // HD
+    me = lax.axis_index("ctx")
+    near = me + 1 - 2 * (me % 2)
+    far = me + 2 - 4 * (me // 2)
+    cross = 3 - me
+    peers = (me, near, far, cross)
+
+    loads = [
+        pltpu.make_async_copy(tok_hbm, tok.at[0], load_sem.at[0]),
+        pltpu.make_async_copy(q_hbm, q_own, load_sem.at[1]),
+        pltpu.make_async_copy(kw_hbm, kw, load_sem.at[2]),
+        pltpu.make_async_copy(vw_hbm, vw, load_sem.at[3]),
+    ]
+    for load in loads:
+        load.start()
+
+    barrier = pltpu.get_barrier_semaphore()
+    for peer in peers[1:]:
+        pl.semaphore_signal(
+            barrier, inc=1, device_id={"ctx": peer}, device_id_type=pl.DeviceIdType.MESH
+        )
+    pl.semaphore_wait(barrier, 3)
+
+    def send(source, target, send_sem, recv_sem, peer):
+        return pltpu.make_async_remote_copy(
+            src_ref=source,
+            dst_ref=target,
+            send_sem=send_sem,
+            recv_sem=recv_sem,
+            device_id={"ctx": peer},
+            device_id_type=pl.DeviceIdType.MESH,
+        )
+
+    step = rows // TOK_CHUNKS
+    far_copies = []
+    relay_copies = []
+    for c in range(TOK_CHUNKS):
+        part = pl.ds(c * step, step)
+        far_copies.append(
+            send(tok_hbm.at[part], tok.at[2, part], tok_send.at[c], tok_recv.at[c], far)
+        )
+        relay_copies.append(
+            send(tok.at[2, part], tok.at[3, part], relay_send.at[c], relay_recv.at[c], near)
+        )
+        far_copies[c].start()
+    near_copy = send(tok_hbm, tok.at[1], near_send.at[0], near_recv.at[0], near)
+    near_copy.start()
+
+    def two_blocks(source, to):
+        count = jnp.int32(0)
+        first = jnp.int32(0)
+        second = jnp.int32(0)
+        for b in range(BLOCKS_DEV):
+            hit = dest[source * BLOCKS_DEV + b] // BLOCKS_DEV == to
+            first = jnp.where(hit & (count == 0), b, first)
+            second = jnp.where(hit & (count == 1), b, second)
+            count = count + hit.astype(jnp.int32)
+        return first, second
+
+    loads[1].wait()
+    qw = width // Q_CHUNKS
+    q_copies = {}
+    pair = 2 * block_rows
+
+    def pick(shape, pieces, wanted):
+        row = lax.broadcasted_iota(jnp.int32, (block_rows, shape), 0)
+        column = lax.broadcasted_iota(jnp.int32, (block_rows, shape), 1)
+        return jnp.concatenate(
+            [jnp.where(row + wanted[p] * block_rows == column, 1.0, 0.0) for p in range(pieces)],
+            axis=0,
+        ).astype(jnp.bfloat16)
+
+    wanted = []
+    for r in range(4):
+        wanted.extend(two_blocks(me, peers[r]))
+    chosen = pick(rows, 8, wanted)
+    for c in range(Q_CHUNKS):
+        packed = jnp.dot(
+            chosen, q_own[:, c * qw : (c + 1) * qw], preferred_element_type=jnp.float32
+        ).astype(jnp.bfloat16)
+        q_all[c, 0] = packed[:pair]
+        q_send[c] = packed[pair:].reshape(3, pair, qw)
+        for r in (1, 3, 2):
+            q_copies[c, r] = send(
+                q_send.at[c, r - 1],
+                q_all.at[c, r],
+                q_ssem.at[c, r - 1],
+                q_rsem.at[c, r - 1],
+                peers[r],
+            )
+            q_copies[c, r].start()
+
+    bounds = []
+    running = jnp.int32(0)
+    for c in range(lengths.shape[0]):
+        running = running + lengths[c]
+        bounds.append(running)
+
+    def clip_of(position):
+        total = jnp.zeros_like(position)
+        for bound in bounds:
+            total = total + jnp.where(position >= bound, 1, 0)
+        return total
+
+    col = lax.broadcasted_iota(jnp.int32, (1, seq), 1)
+    slot = col // rows
+    owner = jnp.where(
+        slot == 0, me, jnp.where(slot == 1, near, jnp.where(slot == 2, far, cross))
+    )
+    key_pos = owner * rows + col % rows
+    key_clip = clip_of(key_pos)
+    key_block = key_pos // block_rows
+    bi = lax.broadcasted_iota(jnp.int32, (blocks, blocks), 0)
+    bj = lax.broadcasted_iota(jnp.int32, (blocks, blocks), 1)
+    link = jnp.where((bi == bj) | (mask_ref[...] == 1), 1.0, 0.0).astype(jnp.bfloat16)
+    spread = jnp.where(
+        lax.broadcasted_iota(jnp.int32, (blocks, seq), 0) == key_block, 1.0, 0.0
+    ).astype(jnp.bfloat16)
+    linked[...] = jnp.dot(link, spread, preferred_element_type=jnp.float32).astype(jnp.bfloat16)
+
+    def blocked_for(first):
+        of_block = []
+        clips = []
+        for r in (first, first + 1):
+            for place in two_blocks(peers[r], me):
+                block = peers[r] * BLOCKS_DEV + place
+                ids = lax.broadcasted_iota(jnp.int32, (block_rows, blocks), 1)
+                of_block.append(jnp.where(ids == block, 1.0, 0.0))
+                clips.append(
+                    clip_of(
+                        block * block_rows
+                        + lax.broadcasted_iota(jnp.int32, (block_rows, 1), 0)
+                    )
+                )
+        seen = jnp.dot(
+            jnp.concatenate(of_block, axis=0).astype(jnp.bfloat16),
+            linked[...],
+            preferred_element_type=jnp.float32,
+        )
+        return (seen < 0.5) | (jnp.concatenate(clips, axis=0) != key_clip)
+
+    def project(first, part, parts):
+        cw = width // parts
+        x = tok[first : first + 2].reshape(2 * rows, width)
+        at = slice(first * rows, (first + 2) * rows)
+        cols = slice(part * cw, (part + 1) * cw)
+        for w, kept in ((kw, keys), (vw, values)):
+            kept[at, cols] = jnp.dot(
+                x, w[:, cols], preferred_element_type=jnp.float32
+            ).astype(jnp.bfloat16)
+
+    def attend(first, blocked, chunk):
+        for h in range(heads // Q_CHUNKS):
+            q = q_all[chunk, first : first + 2, :, h * HD : (h + 1) * HD].reshape(
+                4 * block_rows, HD
+            )
+            at = chunk * qw + h * HD
+            s = lax.dot_general(
+                q, keys[:, at : at + HD], (((1,), (1,)), ((), ())),
+                preferred_element_type=jnp.float32,
+            )
+            s = jnp.where(blocked, -jnp.inf, s)
+            top = jnp.max(s, axis=1, keepdims=True)
+            e = jnp.exp2((s - top) * (LOG2E / HD**0.5))
+            total = jnp.sum(e, axis=1, keepdims=True)
+            mixed = jnp.dot(
+                e.astype(jnp.bfloat16), values[:, at : at + HD],
+                preferred_element_type=jnp.float32,
+            )
+            result[first * 2 * block_rows : (first + 2) * 2 * block_rows, at : at + HD] = (
+                mixed / total
+            ).astype(jnp.bfloat16)
+
+    near_blocked = blocked_for(0)
+    far_blocked = blocked_for(2)
+
+    loads[0].wait()
+    loads[2].wait()
+    loads[3].wait()
+    near_copy.wait_recv()
+    for c in range(TOK_CHUNKS):
+        project(0, c, TOK_CHUNKS)
+        far_copies[c].wait_recv()
+        relay_copies[c].start()
+    for c in range(TOK_CHUNKS):
+        relay_copies[c].wait_recv()
+    for c in range(TOK_CHUNKS):
+        project(2, c, TOK_CHUNKS)
+    for c in range(Q_CHUNKS):
+        q_copies[c, 1].wait_recv()
+        attend(0, near_blocked, c)
+    for c in range(Q_CHUNKS):
+        q_copies[c, 2].wait_recv()
+        q_copies[c, 3].wait_recv()
+        attend(2, far_blocked, c)
+
+    wanted = []
+    for t in range(BLOCKS_DEV):
+        place = jnp.int32(0)
+        for r in range(4):
+            rank = jnp.int32(0)
+            for b in range(BLOCKS_DEV):
+                target = dest[peers[r] * BLOCKS_DEV + b]
+                hit = target == me * BLOCKS_DEV + t
+                place = jnp.where(hit, 2 * r + rank, place)
+                rank = rank + (target // BLOCKS_DEV == me).astype(jnp.int32)
+        wanted.append(place)
+    chosen = pick(2 * rows, BLOCKS_DEV, wanted)
+    out_ref[...] = jnp.dot(chosen, result[...], preferred_element_type=jnp.float32).astype(
+        jnp.bfloat16
+    )
+
+    near_copy.wait_send()
+    for c in range(TOK_CHUNKS):
+        far_copies[c].wait_send()
+        relay_copies[c].wait_send()
+    for c in q_copies.values():
+        c.wait_send()
+
+
+def fused(tokens, queries, key_weight, value_weight, lengths, dest_slot, block_mask):
+    rows, width = tokens.shape
+    seq = 4 * rows
+    pair = rows // 2
+    bf = jnp.bfloat16
+    dma = pltpu.SemaphoreType.DMA
+    qw = width // Q_CHUNKS
+    smem = pl.BlockSpec(memory_space=pltpu.SMEM)
+    vmem = pl.BlockSpec(memory_space=pltpu.VMEM)
+    hbm = pl.BlockSpec(memory_space=pl.ANY)
+    return pl.pallas_call(
+        fused_kernel,
+        out_shape=jax.ShapeDtypeStruct((rows, width), bf),
+        in_specs=[smem, smem, vmem, hbm, hbm, hbm, hbm],
+        out_specs=vmem,
+        scratch_shapes=[
+            pltpu.VMEM((4, rows, width), bf),
+            pltpu.VMEM((rows, width), bf),
+            pltpu.VMEM((Q_CHUNKS, 3, pair, qw), bf),
+            pltpu.VMEM((Q_CHUNKS, 4, pair, qw), bf),
+            pltpu.VMEM(key_weight.shape, bf),
+            pltpu.VMEM(value_weight.shape, bf),
+            pltpu.VMEM((seq, width), bf),
+            pltpu.VMEM((seq, width), bf),
+            pltpu.VMEM((4 * BLOCKS_DEV, seq), bf),
+            pltpu.VMEM((2 * rows, width), bf),
+            dma((4,)),
+            dma((TOK_CHUNKS,)),
+            dma((TOK_CHUNKS,)),
+            dma((TOK_CHUNKS,)),
+            dma((TOK_CHUNKS,)),
+            dma((1,)),
+            dma((1,)),
+            dma((Q_CHUNKS, 3)),
+            dma((Q_CHUNKS, 3)),
+        ],
+        compiler_params=pltpu.CompilerParams(
+            collective_id=0, has_side_effects=True, vmem_limit_bytes=40 * 2**20
+        ),
+        cost_estimate=pl.CostEstimate(
+            flops=2800000000, bytes_accessed=6000000, transcendentals=1100000
+        ),
+    )(dest_slot, lengths, block_mask, tokens, queries, key_weight, value_weight)
+
+
 def solution(mesh):
     placed = (
         P(("dp", "ctx"), None),
@@ -110,5 +416,6 @@
         P("dp", None),
     )
     return jax.shard_map(
-        on_device, mesh=mesh, in_specs=placed, out_specs=P(("dp", "ctx"), None), check_vma=False
-    )
+        fused if mesh.shape["ctx"] == 4 else on_device,
+        mesh=mesh, in_specs=placed, out_specs=P(("dp", "ctx"), None), check_vma=False
+    )

time: 95 us -> 26.5 us (0.28)
  waiting for transfers between devices: 49.5 us -> 0 us
  Pallas kernels: 0 us -> 18.4 us
  between operations: 13.3 us -> 0.02 us
  other arithmetic: 12.1 us -> 0 us
  matrix products: 8.77 us -> 0 us
  local copies, waits for them, and re-layouts: 10.6 us -> 7.79 us
    all_gather x4 -> x0, waiting for transfers between devices: 48.1 us -> none  [the longest x1 17.9 us: on_device(): lax.all_gather(tokens, 'ctx', axis=0, tiled=True)]
    pallas_call x0 -> x1, Pallas kernels: none -> 18.4 us  [fused(): pl.pallas_call(fused_kernel, out_shape=jax.ShapeDtypeStruct((rows, width)...]
    dot_general x5 -> x0, matrix products: 8.77 us -> none  [the longest x1 2.82 us: on_device(): jnp.dot(moved_tokens, value_weight, preferred_element_type=jnp.float32)]
    unnamed x8 -> x15, local copies, waits for them, and re-layouts: 1.35 us -> 7.79 us
    gather x4 -> x0, local copies, waits for them, and re-layouts: 6.16 us -> none  [the longest x2 4.8 us: collect_rows(): jnp.take(piece, position, axis=0)]
    add x2 -> x0, other arithmetic: 5.72 us -> none  [the longest x1 5.64 us: on_device(): key_pos = key_block * block_rows + key_slot % block_rows]
    gather x12 -> x0, other arithmetic: 4.61 us -> none  [the longest x10 4.6 us: on_device(): key_block = source_block[key_slot // block_rows]]
    reshape x1 -> x0, local copies, waits for them, and re-layouts: 1.49 us -> none  [on_device(): value_piece.reshape(count, HEADS, HD)]
  transfers between devices with their start and end apart: 4 -> 0, of which waited for: 3 -> 0; matrix products, arithmetic and copies ran while one was open for 27% -> 0% of each run, Pallas kernels for 0% -> 0%
where the time goes in v1:
time: 26.5 us; the launch traced here: 26.2 us
  Pallas kernels  18.4 us (69%)
  local copies, waits for them, and re-layouts  7.79 us (29%)
    pallas_call x1, Pallas kernels, fused(): pl.pallas_call(fused_kernel, out_shape=jax.ShapeDtypeStruct((rows, width)...  18.4 us
    unnamed x15, local copies, waits for them, and re-layouts  7.79 us

profile of v1, /device:TPU:1, one launch (start us, length us, event | category | flops | bytes accessed | tf_op | source)
XLA Modules:
  0.0 26.2 jit_solution(3715649843923249501)
XLA Ops:
  0.0 0.0 copy-start
  0.0 1.6 %copy-done = bf16[1024,1024]{1,0:T(8,128)(2,1)S(1)} copy-done((bf16[1024,1024]{1,0:T(8,128)(2,1)S(1)}, bf16[1024,1024]{1,0:T(8,128)(2,1)}, u32[]{:S(2)}) %copy-start) | copy-done | bytes 2097176
  1.6 0.0 copy-start.1
  1.6 1.6 %copy-done.1 = bf16[1024,1024]{1,0:T(8,128)(2,1)S(1)} copy-done((bf16[1024,1024]{1,0:T(8,128)(2,1)S(1)}, bf16[1024,1024]{1,0:T(8,128)(2,1)}, u32[]{:S(2)}) %copy-start.1) | copy-done | bytes 2097176
  3.2 0.0 copy-start.2
  3.2 0.9 %copy-done.2 = bf16[128,1024]{1,0:T(8,128)(2,1)S(1)} copy-done((bf16[128,1024]{1,0:T(8,128)(2,1)S(1)}, bf16[128,1024]{1,0:T(8,128)(2,1)}, u32[]{:S(2)}) %copy-start.2) | copy-done | bytes 262168
  4.1 0.0 copy-start.3
  4.1 0.9 %copy-done.3 = bf16[128,1024]{1,0:T(8,128)(2,1)S(1)} copy-done((bf16[128,1024]{1,0:T(8,128)(2,1)S(1)}, bf16[128,1024]{1,0:T(8,128)(2,1)}, u32[]{:S(2)}) %copy-start.3) | copy-done | bytes 262168
  5.1 0.0 copy-start.4
  5.1 0.7 %copy-done.4 = s32[16,16]{1,0:T(8,128)S(1)} copy-done((s32[16,16]{1,0:T(8,128)S(1)}, s32[16,16]{1,0:T(8,128)}, u32[]{:S(2)}) %copy-start.4) | copy-done | bytes 1048
  5.8 0.0 copy-start.5
  5.8 0.7 %copy-done.5 = s32[16]{0:T(128)S(1)} copy-done((s32[16]{0:T(128)S(1)}, s32[16]{0:T(128)}, u32[]{:S(2)}) %copy-start.5) | copy-done | bytes 88
  6.4 0.0 copy-start.6
  6.4 0.7 %copy-done.6 = s32[6]{0:T(128)S(1)} copy-done((s32[6]{0:T(128)S(1)}, s32[6]{0:T(128)}, u32[]{:S(2)}) %copy-start.6) | copy-done | bytes 48
  7.1 18.4 %shard_map.73 = bf16[128,1024]{1,0:T(8,128)(2,1)S(1)} custom-call(s32[16]{0:T(128)S(1)} %copy-done.5, s32[6]{0:T(128)S(1)} %copy-done.6, s32[16,16]{1,0:T(8,128)S(1)} %copy-done.4, bf16[128,1024]{1,0:T(8,128)(2,1)S(1)} %copy-done.2, bf16[128,1024]{1,0:T(8,128)(2,1)S(1)} %copy-done.3, bf16[1024,1024]{1,0:T(8,128)(2,1)S(1)} %copy-done, ...), custom_call_target="tpu_custom_call" | custom-call | flops 2800000000 | bytes 6000000 | tf_op jit(solution)/shard_map/pallas_call | solution.py:373
  25.5 0.7 %copy.9 = bf16[128,1024]{1,0:T(8,128)(2,1)} copy(bf16[128,1024]{1,0:T(8,128)(2,1)S(1)} %shard_map.73) | data formatting | bytes 524288
Async XLA Ops:
  0.0 1.6 %copy-start = (bf16[1024,1024]{1,0:T(8,128)(2,1)S(1)}, bf16[1024,1024]{1,0:T(8,128)(2,1)}, u32[]{:S(2)}) copy-start(bf16[1024,1024]{1,0:T(8,128)(2,1)} %kw_hbm.1) | copy-start | bytes 6291460
  1.6 1.6 %copy-start.1 = (bf16[1024,1024]{1,0:T(8,128)(2,1)S(1)}, bf16[1024,1024]{1,0:T(8,128)(2,1)}, u32[]{:S(2)}) copy-start(bf16[1024,1024]{1,0:T(8,128)(2,1)} %vw_hbm.1) | copy-start | bytes 6291460
  3.2 0.9 %copy-start.2 = (bf16[128,1024]{1,0:T(8,128)(2,1)S(1)}, bf16[128,1024]{1,0:T(8,128)(2,1)}, u32[]{:S(2)}) copy-start(bf16[128,1024]{1,0:T(8,128)(2,1)} %tok_hbm.1) | copy-start | bytes 786436
  4.1 0.9 %copy-start.3 = (bf16[128,1024]{1,0:T(8,128)(2,1)S(1)}, bf16[128,1024]{1,0:T(8,128)(2,1)}, u32[]{:S(2)}) copy-start(bf16[128,1024]{1,0:T(8,128)(2,1)} %q_hbm.1) | copy-start | bytes 786436
  5.1 0.7 %copy-start.4 = (s32[16,16]{1,0:T(8,128)S(1)}, s32[16,16]{1,0:T(8,128)}, u32[]{:S(2)}) copy-start(s32[16,16]{1,0:T(8,128)} %mask_ref.1) | copy-start | bytes 3076
  5.8 0.7 %copy-start.5 = (s32[16]{0:T(128)S(1)}, s32[16]{0:T(128)}, u32[]{:S(2)}) copy-start(s32[16]{0:T(128)} %dest.1) | copy-start | bytes 196
  6.4 0.7 %copy-start.6 = (s32[6]{0:T(128)S(1)}, s32[6]{0:T(128)}, u32[]{:S(2)}) copy-start(s32[6]{0:T(128)} %lengths.1) | copy-start | bytes 76

commit v2 on v1

--- a/solution.py
+++ b/solution.py
@@ -328,14 +328,6 @@
         relay_copies[c].wait_recv()
     for c in range(TOK_CHUNKS):
         project(2, c, TOK_CHUNKS)
-    for c in range(Q_CHUNKS):
-        q_copies[c, 1].wait_recv()
-        attend(0, near_blocked, c)
-    for c in range(Q_CHUNKS):
-        q_copies[c, 2].wait_recv()
-        q_copies[c, 3].wait_recv()
-        attend(2, far_blocked, c)
-
     wanted = []
     for t in range(BLOCKS_DEV):
         place = jnp.int32(0)
@@ -348,9 +340,16 @@
                 rank = rank + (target // BLOCKS_DEV == me).astype(jnp.int32)
         wanted.append(place)
     chosen = pick(2 * rows, BLOCKS_DEV, wanted)
-    out_ref[...] = jnp.dot(chosen, result[...], preferred_element_type=jnp.float32).astype(
-        jnp.bfloat16
-    )
+    for c in range(Q_CHUNKS):
+        q_copies[c, 1].wait_recv()
+        attend(0, near_blocked, c)
+    for c in range(Q_CHUNKS):
+        q_copies[c, 2].wait_recv()
+        q_copies[c, 3].wait_recv()
+        attend(2, far_blocked, c)
+        out_ref[:, c * qw : (c + 1) * qw] = jnp.dot(
+            chosen, result[:, c * qw : (c + 1) * qw], preferred_element_type=jnp.float32
+        ).astype(jnp.bfloat16)
 
     near_copy.wait_send()
     for c in range(TOK_CHUNKS):
@@ -372,7 +371,7 @@
     hbm = pl.BlockSpec(memory_space=pl.ANY)
     return pl.pallas_call(
         fused_kernel,
-        out_shape=jax.ShapeDtypeStruct((rows, width), bf),
+        out_shape=pltpu.VMEM((rows, width), bf),
         in_specs=[smem, smem, vmem, hbm, hbm, hbm, hbm],
         out_specs=vmem,
         scratch_shapes=[
@@ -397,7 +396,7 @@
             dma((Q_CHUNKS, 3)),
         ],
         compiler_params=pltpu.CompilerParams(
-            collective_id=0, has_side_effects=True, vmem_limit_bytes=40 * 2**20
+            collective_id=0, has_side_effects=True, vmem_limit_bytes=58 * 2**20
         ),
         cost_estimate=pl.CostEstimate(
             flops=2800000000, bytes_accessed=6000000, transcendentals=1100000

time: 26.5 us -> 19.6 us (0.74)
  local copies, waits for them, and re-layouts: 7.79 us -> 0.71 us
  Pallas kernels: 18.4 us -> 18.7 us
    unnamed x15 -> x1, local copies, waits for them, and re-layouts: 7.79 us -> 0.71 us
    pallas_call x1, Pallas kernels: 18.4 us -> 18.7 us  [fused(): pl.pallas_call(fused_kernel, out_shape=pltpu.VMEM((rows, width), bf), in_...]
where the time goes in v2:
time: 19.6 us; the launch traced here: 19.4 us
  Pallas kernels  18.7 us (95%)
  local copies, waits for them, and re-layouts  0.71 us (4%)
    pallas_call x1, Pallas kernels, fused(): pl.pallas_call(fused_kernel, out_shape=pltpu.VMEM((rows, width), bf), in_...  18.7 us
    unnamed x1, local copies, waits for them, and re-layouts  0.71 us

profile of v2, /device:TPU:1, one launch (start us, length us, event | category | flops | bytes accessed | tf_op | source)
XLA Modules:
  0.0 19.4 jit_solution(10142657127546280479)
XLA Ops:
  0.0 18.7 %shard_map.73 = bf16[128,1024]{1,0:T(8,128)(2,1)S(1)} custom-call(s32[16]{0:T(128)} %dest.1, s32[6]{0:T(128)} %lengths.1, s32[16,16]{1,0:T(8,128)} %mask_ref.1, bf16[128,1024]{1,0:T(8,128)(2,1)} %tok_hbm.1, bf16[128,1024]{1,0:T(8,128)(2,1)} %q_hbm.1, bf16[1024,1024]{1,0:T(8,128)(2,1)} %kw_hbm.1, bf16[1024,1024]{1,0:T(8,128)(2,1)} %vw_hbm.1), custom_call_target="tpu_custom_call" | custom-call | flops 2800000000 | bytes 6000000 | tf_op jit(solution)/shard_map/pallas_call | solution.py:372
  18.7 0.7 %copy.9 = bf16[128,1024]{1,0:T(8,128)(2,1)} copy(bf16[128,1024]{1,0:T(8,128)(2,1)S(1)} %shard_map.73) | data formatting | bytes 524288

commit v3 on v2

--- a/solution.py
+++ b/solution.py
@@ -104,6 +104,8 @@
 
 TOK_CHUNKS = 4
 Q_CHUNKS = 2
+Q_EARLY = 0
+Q_AFTER = {1: (0,), 3: (1,)}
 LOG2E = 1.4426950408889634
 
 
@@ -125,6 +127,7 @@
     keys,
     values,
     linked,
+    bias,
     result,
     load_sem,
     tok_send,
@@ -230,7 +233,8 @@
                 q_rsem.at[c, r - 1],
                 peers[r],
             )
-            q_copies[c, r].start()
+            if r == 1 or c < Q_EARLY:
+                q_copies[c, r].start()
 
     bounds = []
     running = jnp.int32(0)
@@ -281,17 +285,17 @@
         )
         return (seen < 0.5) | (jnp.concatenate(clips, axis=0) != key_clip)
 
-    def project(first, part, parts):
+    def project(first, part, parts, count=2):
         cw = width // parts
-        x = tok[first : first + 2].reshape(2 * rows, width)
-        at = slice(first * rows, (first + 2) * rows)
+        x = tok[first : first + count].reshape(count * rows, width)
+        at = slice(first * rows, (first + count) * rows)
         cols = slice(part * cw, (part + 1) * cw)
         for w, kept in ((kw, keys), (vw, values)):
             kept[at, cols] = jnp.dot(
                 x, w[:, cols], preferred_element_type=jnp.float32
             ).astype(jnp.bfloat16)
 
-    def attend(first, blocked, chunk):
+    def attend(first, chunk):
         for h in range(heads // Q_CHUNKS):
             q = q_all[chunk, first : first + 2, :, h * HD : (h + 1) * HD].reshape(
                 4 * block_rows, HD
@@ -301,7 +305,7 @@
                 q, keys[:, at : at + HD], (((1,), (1,)), ((), ())),
                 preferred_element_type=jnp.float32,
             )
-            s = jnp.where(blocked, -jnp.inf, s)
+            s = s + bias[first // 2]
             top = jnp.max(s, axis=1, keepdims=True)
             e = jnp.exp2((s - top) * (LOG2E / HD**0.5))
             total = jnp.sum(e, axis=1, keepdims=True)
@@ -313,8 +317,8 @@
                 mixed / total
             ).astype(jnp.bfloat16)
 
-    near_blocked = blocked_for(0)
-    far_blocked = blocked_for(2)
+    bias[0] = jnp.where(blocked_for(0), -jnp.inf, 0.0)
+    bias[1] = jnp.where(blocked_for(2), -jnp.inf, 0.0)
 
     loads[0].wait()
     loads[2].wait()
@@ -324,10 +328,15 @@
         project(0, c, TOK_CHUNKS)
         far_copies[c].wait_recv()
         relay_copies[c].start()
+        for later in Q_AFTER.get(c, ()):
+            q_copies[later, 3].start()
+            q_copies[later, 2].start()
+    for c in range(TOK_CHUNKS):
+        project(2, c, TOK_CHUNKS, 1)
     for c in range(TOK_CHUNKS):
         relay_copies[c].wait_recv()
     for c in range(TOK_CHUNKS):
-        project(2, c, TOK_CHUNKS)
+        project(3, c, TOK_CHUNKS, 1)
     wanted = []
     for t in range(BLOCKS_DEV):
         place = jnp.int32(0)
@@ -342,11 +351,11 @@
     chosen = pick(2 * rows, BLOCKS_DEV, wanted)
     for c in range(Q_CHUNKS):
         q_copies[c, 1].wait_recv()
-        attend(0, near_blocked, c)
+        attend(0, c)
     for c in range(Q_CHUNKS):
         q_copies[c, 2].wait_recv()
         q_copies[c, 3].wait_recv()
-        attend(2, far_blocked, c)
+        attend(2, c)
         out_ref[:, c * qw : (c + 1) * qw] = jnp.dot(
             chosen, result[:, c * qw : (c + 1) * qw], preferred_element_type=jnp.float32
         ).astype(jnp.bfloat16)
@@ -384,6 +393,7 @@
             pltpu.VMEM((seq, width), bf),
             pltpu.VMEM((seq, width), bf),
             pltpu.VMEM((4 * BLOCKS_DEV, seq), bf),
+            pltpu.VMEM((2, rows, seq), jnp.float32),
             pltpu.VMEM((2 * rows, width), bf),
             dma((4,)),
             dma((TOK_CHUNKS,)),

time: 19.6 us -> 19.1 us (0.974)
  Pallas kernels: 18.7 us -> 18.1 us
    pallas_call x1, Pallas kernels: 18.7 us -> 18.1 us  [fused(): pl.pallas_call(fused_kernel, out_shape=pltpu.VMEM((rows, width), bf), in_...]
where the time goes in v3:
time: 19.1 us; the launch traced here: 18.8 us
  Pallas kernels  18.1 us (95%)
  local copies, waits for them, and re-layouts  0.71 us (4%)
    pallas_call x1, Pallas kernels, fused(): pl.pallas_call(fused_kernel, out_shape=pltpu.VMEM((rows, width), bf), in_...  18.1 us
    unnamed x1, local copies, waits for them, and re-layouts  0.71 us

profile of v3, /device:TPU:1, one launch (start us, length us, event | category | flops | bytes accessed | tf_op | source)
XLA Modules:
  0.0 18.8 jit_solution(14349294531992755736)
XLA Ops:
  0.0 18.1 %shard_map.73 = bf16[128,1024]{1,0:T(8,128)(2,1)S(1)} custom-call(s32[16]{0:T(128)} %dest.1, s32[6]{0:T(128)} %lengths.1, s32[16,16]{1,0:T(8,128)} %mask_ref.1, bf16[128,1024]{1,0:T(8,128)(2,1)} %tok_hbm.1, bf16[128,1024]{1,0:T(8,128)(2,1)} %q_hbm.1, bf16[1024,1024]{1,0:T(8,128)(2,1)} %kw_hbm.1, bf16[1024,1024]{1,0:T(8,128)(2,1)} %vw_hbm.1), custom_call_target="tpu_custom_call" | custom-call | flops 2800000000 | bytes 6000000 | tf_op jit(solution)/shard_map/pallas_call | solution.py:381
  18.1 0.7 %copy.9 = bf16[128,1024]{1,0:T(8,128)(2,1)} copy(bf16[128,1024]{1,0:T(8,128)(2,1)S(1)} %shard_map.73) | data formatting | bytes 524288
